TPU v7x, 32 devices: a whole 2x2x4 slice. The times are simulated.
32 devices in a mesh: expert: 8 (over z, x), mp: 4 (over y, core).
Axes of the slice: x: 2, y: 2, z: 4, core: 2. Of those that a mesh axis runs over, the one named last changes fastest.
Arguments:
- stream: bfloat16 [4096, 2048], P(('expert', 'mp')), may hold values from -60 to 60
- attn_gain: float32 [2048], replicated, may hold values from 0.5 to 1.5
- routes: int32 [4096, 6], P(('expert', 'mp')), may hold values from 0 to 15, as said below
- route_weights: float32 [4096, 6], P(('expert', 'mp')), may hold values from 0.05 to 0.4
- segment_ids: int32 [4096], P(('expert', 'mp')), may hold values from 0 to 3, never falling along the last dimension, each value on 1 to 2048 neighbouring positions
- gate_weight: bfloat16 [32, 2048, 704], P(('expert', 'mp')), may hold values from -0.125 to 0.125
- up_weight: bfloat16 [32, 2048, 704], P(('expert', 'mp')), may hold values from -1 to 1
- down_weight: bfloat16 [32, 1408, 1024], P(('expert', 'mp')), may hold values from -0.15625 to 0.15625
- keep_channels: int32 [16, 1024], replicated, may hold values from 0 to 1407, as said below
- next_gain: float32 [2048], replicated, may hold values from 0.5 to 1.5
- kv_down: bfloat16 [2048, 512], replicated, may hold values from -0.125 to 0.125
- rope_down: bfloat16 [2048, 64], replicated, may hold values from -0.125 to 0.125
- kv_gain: float32 [512], replicated, may hold values from 0.5 to 1.5
Outputs:
- moe_out: bfloat16 [4096, 2048], P(('expert', 'mp'))
- latent: bfloat16 [4096, 512], P(('expert', 'mp'))
- rope_key: bfloat16 [4096, 64], P(('expert', 'mp'))
Inputs may be any that keep to these rules, and one draw needn't show every extreme that they name: `routes`: in the 128 rows of each device (aligned blocks of the token order) each row names 6 different experts, no expert is named by more than 72 rows, every expert is named at least once, and one expert, the same on every device, is named by exactly 72 rows. `keep_channels`: each row holds 1024 different hidden units. `segment_ids`: segment ids never fall along the tokens.
All inputs are finite; a program needn't handle non-finite values.
Results may differ from a plain program's by a relative error of at most 0.012.
Values may be sent and summed in bfloat16 or wider, within the bound.
A program may use at most 128 MiB of HBM per device.

v0:
```python
import math

import jax
import jax.numpy as jnp
from jax import lax
from jax.sharding import PartitionSpec as P

TOP = 6


EPSILON = 1e-06
DAMPING = 0.05
ROPE_BASE = 10000.0


def from_partner(value, axis, distance):
    mask = 2**distance
    pairs = [(source, source ^ mask) for source in range(lax.axis_size(axis))]
    return lax.ppermute(value, axis, pairs)


def rms_rows(values, scale_gain):
    mean_square = jnp.mean(values * values, axis=-1, keepdims=True)
    return values * lax.rsqrt(mean_square + EPSILON) * scale_gain


def rotate(rope_in, position):
    half_width = rope_in.shape[1] // 2
    frequency = jnp.exp(
        jnp.arange(half_width, dtype=jnp.float32) * (-2.0 * math.log(ROPE_BASE) / rope_in.shape[1])
    )
    angles = position[:, None] * frequency[None, :]
    first_half = rope_in[:, :half_width]
    second_half = rope_in[:, half_width:]
    cosine = jnp.cos(angles)
    sine = jnp.sin(angles)
    return jnp.concatenate(
        [first_half * cosine - second_half * sine, second_half * cosine + first_half * sine], axis=1
    )


def split_target(cross_gram, down_part):
    cross_high = lax.optimization_barrier(cross_gram.astype(jnp.bfloat16))
    cross_low = (cross_gram - cross_high.astype(jnp.float32)).astype(jnp.bfloat16)
    high_part = jnp.dot(cross_high, down_part, preferred_element_type=jnp.float32)
    low_part = jnp.dot(cross_low, down_part, preferred_element_type=jnp.float32)
    return high_part + low_part


def local(
    stream,
    attn_gain,
    routes,
    route_weights,
    segment_ids,
    gate_weight,
    up_weight,
    down_weight,
    keep_channels,
    next_gain,
    kv_down,
    rope_down,
    kv_gain,
):
    tok_rows = stream.shape[0]
    model_width = stream.shape[1]
    half_width = down_weight.shape[2]
    devices = lax.axis_size(("expert", "mp"))
    experts = devices // 2
    capacity = max(2, 3 * tok_rows * TOP // (2 * experts))
    stream_f = stream.astype(jnp.float32)
    moe_input = rms_rows(stream_f, attn_gain).astype(jnp.bfloat16)
    flat_ids = routes.reshape(-1)
    expert_hits = (flat_ids[:, None] == jnp.arange(experts, dtype=jnp.int32)[None, :]).astype(
        jnp.int32
    )
    earlier = jnp.cumsum(expert_hits, axis=0) - expert_hits
    slot_of = jnp.sum(earlier * expert_hits, axis=1)
    target_slot = flat_ids * capacity + slot_of
    token_of = jnp.arange(tok_rows * TOP, dtype=jnp.int32) // TOP
    source_token = jnp.zeros((experts * capacity,), jnp.int32).at[target_slot].set(token_of)
    filled = jnp.zeros((experts * capacity,), jnp.bfloat16).at[target_slot].set(1.0)
    packed = jnp.take(moe_input, source_token, axis=0) * filled[:, None]
    packed = packed.reshape(experts, capacity, model_width)
    outgoing = jnp.repeat(packed, 2, axis=0)
    block_rows = lax.all_to_all(outgoing, ("expert", "mp"), split_axis=0, concat_axis=0, tiled=True)
    gate_proj = jnp.einsum(
        "...d,df->...f", block_rows, gate_weight[0], preferred_element_type=jnp.float32
    )
    up_proj = jnp.einsum(
        "...d,df->...f", block_rows, up_weight[0], preferred_element_type=jnp.float32
    )
    hidden_mine = (jax.nn.silu(gate_proj) * up_proj).astype(jnp.bfloat16)
    hidden_mine = hidden_mine.reshape(devices * capacity, hidden_mine.shape[-1])
    half_index = lax.axis_index("mp") % 2
    lower_half = half_index == 0
    partner = from_partner(hidden_mine, "mp", 0)
    hidden_all = jnp.where(
        lower_half,
        jnp.concatenate([hidden_mine, partner], axis=1),
        jnp.concatenate([partner, hidden_mine], axis=1),
    )
    expert_id = lax.axis_index(("expert", "mp")) // 2
    kept_index = lax.dynamic_slice_in_dim(keep_channels, expert_id, 1, 0)[0]
    kept = jnp.take(hidden_all, kept_index, axis=1)
    contract_dims = (((0,), (0,)), ((), ()))
    cross_gram = lax.dot_general(
        kept, hidden_all, contract_dims, preferred_element_type=jnp.float32
    )
    inner_gram = jnp.take(cross_gram, kept_index, axis=1)
    damping_term = DAMPING * jnp.mean(jnp.diagonal(inner_gram))
    system = inner_gram + damping_term * jnp.eye(inner_gram.shape[0], dtype=jnp.float32)
    factor = jnp.linalg.cholesky(system)
    target_cols = split_target(cross_gram, down_weight[0])
    pruned = jax.scipy.linalg.cho_solve((factor, True), target_cols).astype(jnp.bfloat16)
    refit = jnp.dot(kept, pruned, preferred_element_type=jnp.float32).astype(jnp.bfloat16)
    refit = refit.reshape(devices, capacity, half_width)
    token_total = tok_rows * devices
    seq_length = min(2048, token_total // 2)
    sequences = 2 * token_total // seq_length
    seq_hits = segment_ids[:, None] == jnp.arange(sequences, dtype=jnp.int32)[None, :]
    local_counts = jnp.sum(seq_hits.astype(jnp.float32), axis=0)
    counts = lax.psum(local_counts, ("expert", "mp"))
    starts = jnp.cumsum(counts) - counts
    token_start = jnp.sum(jnp.where(seq_hits, starts[None, :], 0.0), axis=1)
    global_index = (
        lax.axis_index(("expert", "mp")) * tok_rows + jnp.arange(tok_rows, dtype=jnp.int32)
    ).astype(jnp.float32)
    position = global_index - token_start
    returned = lax.all_to_all(refit, ("expert", "mp"), split_axis=0, concat_axis=0, tiled=True)
    returned = returned.reshape(experts * 2 * capacity, half_width)
    lower_index = flat_ids * (2 * capacity) + slot_of
    lower_rows = jnp.take(returned, lower_index, axis=0).reshape(tok_rows, TOP, half_width)
    upper_rows = jnp.take(returned, lower_index + capacity, axis=0).reshape(
        tok_rows, TOP, half_width
    )
    weights = route_weights[:, :, None]
    lower_sum = jnp.sum(weights * lower_rows.astype(jnp.float32), axis=1)
    upper_sum = jnp.sum(weights * upper_rows.astype(jnp.float32), axis=1)
    moe_out = jnp.concatenate([lower_sum, upper_sum], axis=1).astype(jnp.bfloat16)
    next_stream = (stream_f + moe_out.astype(jnp.float32)).astype(jnp.bfloat16)
    normed = rms_rows(next_stream.astype(jnp.float32), next_gain).astype(jnp.bfloat16)
    compressed = jnp.dot(normed, kv_down, preferred_element_type=jnp.float32)
    latent = rms_rows(compressed, kv_gain).astype(jnp.bfloat16)
    rope_in = jnp.dot(normed, rope_down, preferred_element_type=jnp.float32)
    rope_key = rotate(rope_in, position).astype(jnp.bfloat16)
    return (moe_out, latent, rope_key)


def solution(mesh):
    in_specs = (
        P(("expert", "mp"), None),
        P(),
        P(("expert", "mp"), None),
        P(("expert", "mp"), None),
        P(("expert", "mp")),
        P(("expert", "mp"), None, None),
        P(("expert", "mp"), None, None),
        P(("expert", "mp"), None, None),
        P(),
        P(),
        P(),
        P(),
        P(),
    )
    out_specs = (P(("expert", "mp"), None), P(("expert", "mp"), None), P(("expert", "mp"), None))
    return jax.shard_map(local, mesh=mesh, in_specs=in_specs, out_specs=out_specs, check_vma=False)
```

profile of v0, /device:TPU:0, one launch (start us, length us, event | category | flops | bytes accessed | tf_op | source)
XLA Modules:
  0.0 909.5 jit_solution(15535559377954499571)
XLA Ops:
  5.0 3.4 scatter_custom_fusion
  9.8 8.6 scatter_custom_fusion.1
  19.8 6.0 gather_fusion
  25.8 5.0 select_multiply_fusion
  30.7 7.5 broadcast_in_dim.97
  38.3 213.5 %all_to_all.10 = bf16[32,72,2048]{2,1,0:T(8,128)(2,1)S(1)} all-to-all(bf16[32,72,2048]{2,1,0:T(8,128)(2,1)} %bitcast.183), channel_id=1, replica_groups=mesh['expert'=8,'mp'=4] {'expert','mp'}, dimensions={0} | all-to-all | bytes 18874368 | tf_op jit(solution)/shard_map/all_to_all | solution.py:86
  251.8 8.3 fusion.4
  260.1 10.2 %multiply_convert_fusion = bf16[32,72,704]{2,1,0:T(8,128)(2,1)} fusion(f32[32,72,704]{2,1,0:T(8,128)S(1)} %fusion.4, bf16[32,72,2048]{2,1,0:T(8,128)(2,1)S(1)} %all_to_all.10, bf16[1,2048,704]{1,2,0:T(8,128)(2,1)S(1)} %copy-done.12), kind=kOutput, calls=%fused_computation.10 | convolution fusion | flops 6653509632 | bytes 22052864 | tf_op jit(solution)/shard_map/...d,df->...f/dot_general | solution.py:87
  270.3 5.7 copy.42
  276.8 5.3 collective-permute-done
  282.1 9.2 %maximum_select_fusion = bf16[2304,1408]{0,1:T(8,128)(2,1)} fusion(bf16[2304,704]{0,1:T(8,128)(2,1)} %collective-permute-done, bf16[2304,704]{0,1:T(8,128)(2,1)} %copy.42, pred[]{:T(512)S(6)} %eq.49), kind=kLoop, calls=%fused_computation.11 | loop fusion | flops 29196288 | bytes 12976129 | tf_op jit(solution)/shard_map/jit(_where)/select_n | solution.py:98
  291.3 13.4 %gather_fusion.1 = bf16[1024,2304]{1,0:T(8,128)(2,1)} fusion(bf16[2304,1408]{0,1:T(8,128)(2,1)} %maximum_select_fusion, s32[1024]{0:T(1024)S(1)} %broadcast_clamp_fusion), kind=kCustom, calls=%fused_computation.3 | custom fusion | bytes 9441280 | tf_op jit(solution)/shard_map/jit(_take)/gather | solution.py:105
  304.7 13.6 %fusion.155 = (bf16[1024,1408]{1,0:T(8,128)(2,1)}, f32[1024,1408]{1,0:T(8,128)}) fusion(bf16[2304,1408]{0,1:T(8,128)(2,1)} %maximum_select_fusion, bf16[1024,2304]{1,0:T(8,128)(2,1)} %gather_fusion.1, pred[1024]{0:T(1024)(128)(4,1)S(1)} %compare_and_fusion.3), kind=kOutput, calls=%fused_computation.326 | convolution fusion | flops 6647578624 | bytes 19858432 | tf_op jit(solution)/shard_map/dot_general | solution.py:107
  318.3 6.3 copy.44
  324.6 9.0 gather_fusion.2
  333.6 4.5 select_bitcast_fusion
  338.2 17.3 %gather_fusion.3 = f32[1024]{0:T(1024)S(1)} fusion(f32[1024,1024]{0,1:T(8,128)} %select_bitcast_fusion, s32[1024]{0:T(1024)S(1)} %bitcast.182), kind=kCustom, calls=%fused_computation.5 | custom fusion | bytes 16384 | tf_op jit(solution)/shard_map/jit(diagonal)/cond/branch_0_fun/gather | solution.py:111
  356.7 4.6 select_add_fusion
  361.3 5.5 copy.47
  366.8 4.0 add_multiply_fusion
  372.9 11.7 %cholesky.221 = f32[128,128]{1,0:T(8,128)S(1)} custom-call(f32[128,128]{1,0:T(8,128)S(1)} %cholesky.574), custom_call_target="Cholesky" | custom-call | tf_op jit(solution)/shard_map/jit(cholesky)/cholesky | solution.py:113
  384.6 2.5 cholesky.251
  387.1 9.8 %custom-call.66 = f32[1,128,128]{1,2,0:T(8,128)S(1)} custom-call(f32[1,128,128]{2,1,0:T(8,128)S(1)} %get-tuple-element.70), custom_call_target="InvertDiagBlocksLowerTriangular" | custom-call | tf_op jit(solution)/shard_map/jit(cholesky)/cholesky | solution.py:113
  396.9 2.3 constant_dynamic-update-slice_fusion.43
  400.8 11.7 %cholesky.242 = f32[128,128]{1,0:T(8,128)S(1)} custom-call(f32[128,128]{1,0:T(8,128)S(1)} %cholesky.578), custom_call_target="Cholesky" | custom-call | tf_op jit(solution)/shard_map/jit(cholesky)/cholesky | solution.py:113
  413.2 9.9 %custom-call.67 = f32[1,128,128]{1,2,0:T(8,128)S(1)} custom-call(f32[1,128,128]{2,1,0:T(8,128)S(1)} %get-tuple-element.67), custom_call_target="InvertDiagBlocksLowerTriangular" | custom-call | tf_op jit(solution)/shard_map/jit(cholesky)/cholesky | solution.py:113
  426.5 11.7 %cholesky.464 = f32[128,128]{1,0:T(8,128)S(1)} custom-call(f32[128,128]{1,0:T(8,128)S(1)} %cholesky.583), custom_call_target="Cholesky" | custom-call | tf_op jit(solution)/shard_map/jit(cholesky)/cholesky | solution.py:113
  439.5 9.8 %custom-call.68 = f32[1,128,128]{1,2,0:T(8,128)S(1)} custom-call(f32[1,128,128]{2,1,0:T(8,128)S(1)} %get-tuple-element.64), custom_call_target="InvertDiagBlocksLowerTriangular" | custom-call | tf_op jit(solution)/shard_map/jit(cholesky)/cholesky | solution.py:113
  450.4 2.3 convolution_subtract_fusion.12
  452.8 12.1 %cholesky.483 = f32[128,128]{1,0:T(8,128)S(1)} custom-call(f32[128,128]{1,0:T(8,128)S(1)} %cholesky.588), custom_call_target="Cholesky" | custom-call | tf_op jit(solution)/shard_map/jit(cholesky)/cholesky | solution.py:113
  466.2 9.8 %custom-call.69 = f32[1,128,128]{1,2,0:T(8,128)S(1)} custom-call(f32[1,128,128]{2,1,0:T(8,128)S(1)} %get-tuple-element.61), custom_call_target="InvertDiagBlocksLowerTriangular" | custom-call | tf_op jit(solution)/shard_map/jit(cholesky)/cholesky | solution.py:113
  477.1 2.3 convolution_subtract_fusion.13
  479.5 11.7 %cholesky.502 = f32[128,128]{1,0:T(8,128)S(1)} custom-call(f32[128,128]{1,0:T(8,128)S(1)} %cholesky.593), custom_call_target="Cholesky" | custom-call | tf_op jit(solution)/shard_map/jit(cholesky)/cholesky | solution.py:113
  492.5 9.8 %custom-call.70 = f32[1,128,128]{1,2,0:T(8,128)S(1)} custom-call(f32[1,128,128]{2,1,0:T(8,128)S(1)} %get-tuple-element.58), custom_call_target="InvertDiagBlocksLowerTriangular" | custom-call | tf_op jit(solution)/shard_map/jit(cholesky)/cholesky | solution.py:113
  503.4 2.3 convolution_subtract_fusion.14
  505.7 11.7 %cholesky.522 = f32[128,128]{1,0:T(8,128)S(1)} custom-call(f32[128,128]{1,0:T(8,128)S(1)} %cholesky.598), custom_call_target="Cholesky" | custom-call | tf_op jit(solution)/shard_map/jit(cholesky)/cholesky | solution.py:113
  518.7 9.8 %custom-call.71 = f32[1,128,128]{1,2,0:T(8,128)S(1)} custom-call(f32[1,128,128]{2,1,0:T(8,128)S(1)} %get-tuple-element.55), custom_call_target="InvertDiagBlocksLowerTriangular" | custom-call | tf_op jit(solution)/shard_map/jit(cholesky)/cholesky | solution.py:113
  531.6 11.7 %cholesky.542 = f32[128,128]{1,0:T(8,128)S(1)} custom-call(f32[128,128]{1,0:T(8,128)S(1)} %cholesky.603), custom_call_target="Cholesky" | custom-call | tf_op jit(solution)/shard_map/jit(cholesky)/cholesky | solution.py:113
  544.7 10.0 %custom-call.72 = f32[1,128,128]{1,2,0:T(8,128)S(1)} custom-call(f32[1,128,128]{2,1,0:T(8,128)S(1)} %get-tuple-element.52), custom_call_target="InvertDiagBlocksLowerTriangular" | custom-call | tf_op jit(solution)/shard_map/jit(cholesky)/cholesky | solution.py:113
  557.3 11.7 %cholesky.560 = f32[128,128]{1,0:T(8,128)S(1)} custom-call(f32[128,128]{1,0:T(8,128)S(1)} %convolution_subtract_fusion.16), custom_call_target="Cholesky" | custom-call | tf_op jit(solution)/shard_map/jit(cholesky)/cholesky | solution.py:113
  576.0 4.8 select_select_fusion
  580.8 27.6 %while.1 = (s32[]{:T(128)}, f32[1024,1024]{1,0:T(8,128)}, s32[8,2]{0,1:T(2,128)S(1)}, f32[8,128,128]{2,1,0:T(8,128)}, s32[]{:T(128)}) while((s32[]{:T(128)}, f32[1024,1024]{1,0:T(8,128)}, s32[8,2]{0,1:T(2,128)S(1)}, f32[8,128,128]{2,1,0:T(8,128)}, s32[]{:T(128)}) %tuple.73), condition=%wide.while_cond, body=%wide.while_body.sunk | while | flops 2 | bytes 132705 | solution.py:115
  581.5 2.8 bitcast_dynamic-update-slice_fusion.2
  584.9 2.8 bitcast_dynamic-update-slice_fusion.2
  588.4 2.8 bitcast_dynamic-update-slice_fusion.2
  591.8 2.8 bitcast_dynamic-update-slice_fusion.2
  595.3 2.8 bitcast_dynamic-update-slice_fusion.2
  598.7 2.8 bitcast_dynamic-update-slice_fusion.2
  602.2 2.8 bitcast_dynamic-update-slice_fusion.2
  605.6 2.7 bitcast_dynamic-update-slice_fusion.2
  608.4 79.4 %custom-call.73 = f32[8,128,128]{1,2,0:T(8,128)S(1)} custom-call(f32[8,128,128]{2,1,0:T(8,128)} %get-tuple-element.11), custom_call_target="InvertDiagBlocksLowerTriangular" | custom-call | tf_op jit(solution)/shard_map/jit(_cho_solve)/triangular_solve | solution.py:115
  687.8 7.3 fusion
  695.1 3.5 fusion.24
  726.3 2.3 convolution_subtract_fusion.6
  729.5 7.2 convolution_convert_fusion
  736.6 4.0 all-to-all-start.1
  740.7 127.2 %psum.7 = f32[4]{0:T(128)S(1)} all-reduce(f32[4]{0:T(128)S(1)} %convert_reduce_fusion), channel_id=1, replica_groups=mesh['expert'=8,'mp'=4] {'expert','mp'}, use_global_device_ids=true, to_apply=%region_28.30 | all-reduce | flops 4 | bytes 32 | tf_op jit(solution)/shard_map/psum | solution.py:123
  868.4 7.5 gather_fusion.5
  875.9 3.3 select_convert_fusion
  879.2 4.7 reshape.323
  883.9 7.5 gather_fusion.4
  891.4 3.3 select_convert_fusion.1
  894.8 4.6 reshape.322
  899.4 6.8 multiply_reduce_fusion.1
  (189 shorter events, 70.4 us)
Async XLA Ops:
  0.6 687.1 %copy-start = (bf16[1,1408,1024]{2,1,0:T(8,128)(2,1)S(1)}, bf16[1,1408,1024]{2,1,0:T(8,128)(2,1)}, u32[]{:S(2)}) copy-start(bf16[1,1408,1024]{2,1,0:T(8,128)(2,1)} %param.22) | copy-start | bytes 8650756
  1.9 16.5 %copy-start.5 = (s32[768]{0:T(1024)}, s32[768]{0:T(1024)S(1)}, u32[]{:S(2)}) copy-start(s32[768]{0:T(1024)S(1)} %eq.50) | copy-start | bytes 9220
  5.0 13.5 %copy-start.7 = (s32[768]{0:T(1024)}, s32[768]{0:T(1024)S(1)}, u32[]{:S(2)}) copy-start(s32[768]{0:T(1024)S(1)} %fusion.124) | copy-start | bytes 9220
  38.3 213.5 %copy-start.11 = (bf16[1,2048,704]{1,2,0:T(8,128)(2,1)S(1)}, bf16[1,2048,704]{1,2,0:T(8,128)(2,1)}, u32[]{:S(2)}) copy-start(bf16[1,2048,704]{1,2,0:T(8,128)(2,1)} %param.21) | copy-start | bytes 8650756
  251.8 8.3 copy-start.12
  275.9 6.1 collective-permute-start
  370.9 2.0 copy-start.2
  687.8 7.3 copy-start.17
  695.1 4.2 copy-start.1
  726.2 3.2 slice-start
  726.3 3.2 slice-start.1
  736.6 4.0 copy-start.16
  736.6 131.3 %copy-start.9 = (f32[128,6]{0,1:T(8,128)S(1)}, f32[128,6]{0,1:T(8,128)}, u32[]{:S(2)}) copy-start(f32[128,6]{0,1:T(8,128)} %param.18) | copy-start | bytes 9220
  736.6 131.6 %copy-start.6 = (s32[768]{0:T(1024)S(1)}, s32[768]{0:T(1024)}, u32[]{:S(2)}) copy-start(s32[768]{0:T(1024)} %copy-done.5) | copy-start | bytes 9220
  736.6 131.6 %copy-start.8 = (s32[768]{0:T(1024)S(1)}, s32[768]{0:T(1024)}, u32[]{:S(2)}) copy-start(s32[768]{0:T(1024)} %copy-done.7) | copy-start | bytes 9220
  736.6 131.7 %all-to-all-start.1 = ((bf16[32,72,1024]{2,1,0:T(8,128)(2,1)}), bf16[32,72,1024]{2,1,0:T(8,128)(2,1)}, u32[]{:S(2)}, u32[]{:S(2)}) async-start(bf16[32,72,1024]{2,1,0:T(8,128)(2,1)} %bitcast.185), calls=%async_computation.1 | async-start | bytes 9437184 | tf_op jit(solution)/shard_map/all_to_all | solution.py:130
  899.4 6.8 copy-start.3
  899.4 7.1 copy-start.14
  899.4 7.1 copy-start.15
  899.4 7.5 copy-start.13
  906.2 2.1 copy-start.10
  906.5 2.6 copy-start.4
where the time goes:
time: 918 us; the launch traced here: 910 us
  blocking collectives  341 us (37%)
  other arithmetic  306 us (33%)
  local copies, waits for them, and re-layouts  142 us (15%)
  matrix products  104 us (11%)
    all_to_all x1, blocking collectives, local(): lax.all_to_all(outgoing, ('expert', 'mp'), split_axis=0, concat_axis=0, t...  214 us
    another operation x30, other arithmetic, local(): factor = jnp.linalg.cholesky(system)  172 us
    psum x1, blocking collectives, local(): counts = lax.psum(local_counts, ('expert', 'mp'))  127 us
    another operation x4, other arithmetic, local(): jax.scipy.linalg.cho_solve((factor, True), target_cols).astype(jnp.bfloat16)  84.3 us
    another operation x30, matrix products, local(): jax.scipy.linalg.cho_solve((factor, True), target_cols).astype(jnp.bfloat16)  29.7 us
    another operation x25, local copies, waits for them, and re-layouts  27.8 us
    another operation x14, matrix products, local(): factor = jnp.linalg.cholesky(system)  23.3 us
  transfers between devices with their start and end apart: 2, of which 1 were waited for; matrix products, arithmetic and copies ran while one was open for 0% of the time, Pallas kernels for 0%

commit v1 on v0

v1 whole, which is shorter than its diff:
```python
import functools
import math

import jax
import jax.numpy as jnp
from jax import lax
from jax.experimental import pallas as pl
from jax.experimental.pallas import tpu as pltpu
from jax.sharding import Mesh
from jax.sharding import PartitionSpec as P

TOP = 6
EPSILON = 1e-06
DAMPING = 0.05
ROPE_BASE = 10000.0
BLOCK = 128
SUB = 8
CHIPS = ("expert", "y")
DEVICES = ("expert", "y", "core")


def rms_rows(values, scale_gain):
    mean_square = jnp.mean(values * values, axis=-1, keepdims=True)
    return values * lax.rsqrt(mean_square + EPSILON) * scale_gain


def rotate(rope_in, position):
    half_width = rope_in.shape[1] // 2
    frequency = jnp.exp(
        jnp.arange(half_width, dtype=jnp.float32) * (-2.0 * math.log(ROPE_BASE) / rope_in.shape[1])
    )
    angles = position[:, None] * frequency[None, :]
    first_half = rope_in[:, :half_width]
    second_half = rope_in[:, half_width:]
    cosine = jnp.cos(angles)
    sine = jnp.sin(angles)
    return jnp.concatenate(
        [first_half * cosine - second_half * sine, second_half * cosine + first_half * sine], axis=1
    )


def precise_dot(a, b):
    return jnp.dot(a, b, precision=lax.Precision.HIGHEST, preferred_element_type=jnp.float32)


def sweep_panel(panel, row_id, lane_id):
    for q in range(0, SUB, 2):
        c0 = jnp.broadcast_to(panel[:, q : q + 1], panel.shape)
        c1 = jnp.broadcast_to(panel[:, q + 1 : q + 2], panel.shape)
        r0 = jnp.broadcast_to(panel[q : q + 1, :], panel.shape)
        r1 = jnp.broadcast_to(panel[q + 1 : q + 2, :], panel.shape)
        a = jnp.broadcast_to(c0[q : q + 1, :], panel.shape)
        b = jnp.broadcast_to(c1[q : q + 1, :], panel.shape)
        d = jnp.broadcast_to(c1[q + 1 : q + 2, :], panel.shape)
        inverse = 1.0 / (a * d - b * b)
        i00, i01, i11 = d * inverse, -b * inverse, a * inverse
        at0, at1 = lane_id == q, lane_id == q + 1
        r0 = jnp.where(at0, 1.0, jnp.where(at1, 0.0, r0))
        r1 = jnp.where(at1, 1.0, jnp.where(at0, 0.0, r1))
        s0 = i00 * r0 + i01 * r1
        s1 = i01 * r0 + i11 * r1
        swept = jnp.where(at0 | at1, 0.0, panel) - c0 * s0 - c1 * s1
        panel = jnp.where(row_id == q, s0, jnp.where(row_id == q + 1, s1, swept))
    return panel


def sweep_step(rows):
    row_id = lax.broadcasted_iota(jnp.int32, (SUB, BLOCK), 0)
    lane_id = lax.broadcasted_iota(jnp.int32, (SUB, BLOCK), 1)
    done = sweep_panel(rows[0], row_id, lane_id)
    spread = [jnp.broadcast_to(done[q : q + 1, :], done.shape) for q in range(SUB)]
    out = []
    for row in rows[1:]:
        left = jnp.where(lane_id < SUB, 0.0, row)
        terms = [jnp.broadcast_to(row[:, q : q + 1], row.shape) * spread[q] for q in range(SUB)]
        while len(terms) > 1:
            terms = [terms[i] + terms[i + 1] for i in range(0, len(terms), 2)]
        out.append(left - terms[0])
    out.append(done)
    return tuple(pltpu.roll(row, BLOCK - SUB, 1) for row in out)


def solve_kernel(inner_ref, target_ref, out_ref, work, gain):
    size = inner_ref.shape[0]
    width = target_ref.shape[1]
    blocks = size // BLOCK
    eye = lax.broadcasted_iota(jnp.int32, (BLOCK, BLOCK), 0) == lax.broadcasted_iota(
        jnp.int32, (BLOCK, BLOCK), 1
    )
    trace = jnp.zeros((BLOCK, BLOCK), jnp.float32)
    for k in range(blocks):
        at = pl.ds(k * BLOCK, BLOCK)
        trace = trace + jnp.where(eye, inner_ref[at, at], 0.0)
    total = jnp.sum(jnp.sum(trace, axis=1, keepdims=True), axis=0, keepdims=True)
    scale = size / total

    @pl.loop(0, size // 32)
    def _(i):
        at = pl.ds(pl.multiple_of(i * 32, 32), 32)
        work[at, :size] = inner_ref[at, :] * scale
        work[at, size:] = target_ref[at, :] * scale

    for k in range(blocks):
        at = pl.ds(k * BLOCK, BLOCK)
        low = (k + 1) * BLOCK
        square = work[at, at] + jnp.where(eye, DAMPING, 0.0)
        rows = tuple(square[SUB * i : SUB * (i + 1), :] for i in range(BLOCK // SUB))
        rows = lax.fori_loop(0, BLOCK // SUB, lambda _, rows: sweep_step(rows), rows)
        inverse = jnp.concatenate(rows, axis=0)
        tile = 512 if low % 512 == 0 else (256 if low % 256 == 0 else BLOCK)

        def column(start, tile, low=low, at=at, inverse=inverse):
            cols = pl.ds(start, tile)
            solved = precise_dot(inverse, work[at, cols])
            gain[at, cols] = solved
            if low < size:
                work[low:, cols] -= precise_dot(work[low:, at], solved)

        start = low
        while start % 512:
            column(start, BLOCK)
            start += BLOCK

        @pl.loop(0, (size + width - start) // 512)
        def _(i, start=start, column=column):
            column(pl.multiple_of(start + i * 512, 512), 512)

    @pl.loop(0, width // 256)
    def _(i):
        start = pl.multiple_of(i * 256, 256)
        cols = pl.ds(pl.multiple_of(size + start, 256), 256)
        for k in reversed(range(blocks)):
            at = pl.ds(k * BLOCK, BLOCK)
            low = (k + 1) * BLOCK
            value = gain[at, cols]
            if low < size:
                value = value - precise_dot(gain[at, low:size], work[low:, cols])
            work[at, cols] = value
        out_ref[:, pl.ds(start, 256)] = work[:, cols].astype(out_ref.dtype)


def damped_solve(inner, target):
    size, width = inner.shape[0], target.shape[1]
    return pl.pallas_call(
        solve_kernel,
        out_shape=jax.ShapeDtypeStruct((size, width), jnp.bfloat16),
        in_specs=[pl.BlockSpec(memory_space=pltpu.VMEM)] * 2,
        out_specs=pl.BlockSpec(memory_space=pltpu.VMEM),
        scratch_shapes=[
            pltpu.VMEM((size, size + width), jnp.float32),
            pltpu.VMEM((size, size + width), jnp.float32),
        ],
        compiler_params=pltpu.CompilerParams(vmem_limit_bytes=48 * 2**20),
        cost_estimate=pl.CostEstimate(
            flops=6 * size * size * width, bytes_accessed=10 * size * width, transcendentals=0
        ),
    )(inner, target)


def split_target(cross_gram, down_part):
    cross_high = lax.optimization_barrier(cross_gram.astype(jnp.bfloat16))
    cross_low = (cross_gram - cross_high.astype(jnp.float32)).astype(jnp.bfloat16)
    high_part = jnp.dot(cross_high, down_part, preferred_element_type=jnp.float32)
    low_part = jnp.dot(cross_low, down_part, preferred_element_type=jnp.float32)
    return high_part + low_part


def both_halves(value, core):
    other = lax.ppermute(value, "core", [(0, 1), (1, 0)])
    return jnp.where(
        core == 0,
        jnp.concatenate([value, other], axis=1),
        jnp.concatenate([other, value], axis=1),
    )


def local(
    stream,
    attn_gain,
    routes,
    route_weights,
    segment_ids,
    gate_weight,
    up_weight,
    down_weight,
    keep_channels,
    next_gain,
    kv_down,
    rope_down,
    kv_gain,
):
    f32, bf16 = jnp.float32, jnp.bfloat16
    tok_rows = stream.shape[0]
    chips = lax.axis_size(CHIPS)
    devices = 2 * chips
    experts = chips
    capacity = max(2, 3 * tok_rows * TOP // (2 * experts))
    core = lax.axis_index("core")
    expert_id = lax.axis_index(CHIPS)
    stream_f = stream.astype(f32)
    moe_input = rms_rows(stream_f, attn_gain).astype(bf16)
    half_width = down_weight.shape[2]
    model_width = stream.shape[1]

    gathered = lax.all_gather(moe_input, CHIPS, tiled=True).reshape(chips, tok_rows, model_width)
    gate_full = both_halves(gate_weight[0], core)
    up_full = both_halves(up_weight[0], core)

    token_total = tok_rows * devices
    seq_length = min(2048, token_total // 2)
    sequences = 2 * token_total // seq_length
    seq_hits = segment_ids[:, None] == jnp.arange(sequences, dtype=jnp.int32)[None, :]
    local_counts = jnp.sum(seq_hits.astype(f32), axis=0)
    count_row = jnp.pad(local_counts, (0, tok_rows - sequences))[None, :]
    packed_routes = jnp.concatenate([routes.T.astype(f32), route_weights.T, count_row], axis=0)
    all_routes = lax.all_gather(packed_routes, DEVICES)
    chosen = all_routes[:, :TOP] == expert_id.astype(f32)
    weight_rows = jnp.sum(jnp.where(chosen, all_routes[:, TOP : 2 * TOP], 0.0), axis=1)
    hits = jnp.any(chosen, axis=1)
    token_order = jnp.arange(tok_rows, dtype=jnp.int32)
    earlier = (token_order[:, None] < token_order[None, :]).astype(bf16)
    slots = jnp.dot(hits.astype(bf16), earlier, preferred_element_type=f32)
    slots = jnp.where(hits, slots, -1.0)
    slot_ids = jnp.arange(capacity, dtype=jnp.int32).astype(f32)
    by_core = slots.reshape(chips, 2, tok_rows)
    slots_mine = lax.dynamic_index_in_dim(by_core, core, 1, keepdims=False)
    slots_other = lax.dynamic_index_in_dim(by_core, 1 - core, 1, keepdims=False)
    weights_by_core = weight_rows.reshape(chips, 2, tok_rows)

    pick = (slots_mine[:, None, :] == slot_ids[None, :, None]).astype(bf16)
    picked = jnp.einsum("bct,btd->bcd", pick, gathered, preferred_element_type=f32).astype(bf16)
    picked = picked.reshape(chips * capacity, model_width)
    gate_proj = jnp.dot(picked, gate_full, preferred_element_type=f32)
    up_proj = jnp.dot(picked, up_full, preferred_element_type=f32)
    hidden_mine = (jax.nn.silu(gate_proj) * up_proj).astype(bf16)
    hidden_other = lax.ppermute(hidden_mine, "core", [(0, 1), (1, 0)])

    kept_index = lax.dynamic_slice_in_dim(keep_channels, expert_id, 1, 0)[0]
    unit_ids = jnp.arange(hidden_mine.shape[1], dtype=jnp.int32)
    select = (unit_ids[:, None] == kept_index[None, :]).astype(bf16)
    kept_mine = jnp.dot(hidden_mine, select, preferred_element_type=f32).astype(bf16)
    kept_other = jnp.dot(hidden_other, select, preferred_element_type=f32).astype(bf16)
    contract = (((0,), (0,)), ((), ()))
    gram = functools.partial(
        lax.dot_general, dimension_numbers=contract, preferred_element_type=f32
    )
    cross_gram = gram(kept_mine, hidden_mine) + gram(kept_other, hidden_other)
    inner_gram = gram(kept_mine, kept_mine) + gram(kept_other, kept_other)
    target_cols = split_target(cross_gram, down_weight[0])
    pruned = damped_solve(inner_gram, target_cols)

    def weighted(kept, slot_rows, weights):
        refit = jnp.dot(kept, pruned, preferred_element_type=f32).astype(bf16)
        place = slot_rows[:, None, :] == slot_ids[None, :, None]
        slot_weights = jnp.sum(jnp.where(place, weights[:, None, :], 0.0), axis=2)
        rows = refit.astype(f32) * slot_weights.reshape(-1)[:, None]
        return rows.astype(bf16).reshape(chips, capacity, half_width)

    weights_mine = lax.dynamic_index_in_dim(weights_by_core, core, 1, keepdims=False)
    weights_other = lax.dynamic_index_in_dim(weights_by_core, 1 - core, 1, keepdims=False)
    rows_mine = weighted(kept_mine, slots_mine, weights_mine)
    rows_other = weighted(kept_other, slots_other, weights_other)
    outgoing = jnp.stack(
        [jnp.where(core == 0, rows_mine, rows_other), jnp.where(core == 0, rows_other, rows_mine)],
        axis=1,
    ).reshape(devices, capacity, half_width)
    returned = lax.all_to_all(outgoing, DEVICES, split_axis=0, concat_axis=0, tiled=True)
    returned = returned.reshape(experts, 2, capacity, half_width)
    expert_range = jnp.arange(experts, dtype=jnp.int32)
    local_hits = jnp.any(routes[:, :, None] == expert_range[None, None, :], axis=1)
    local_slots = jnp.dot(earlier.T, local_hits.astype(bf16), preferred_element_type=f32)
    local_slots = jnp.where(local_hits, local_slots, -1.0)
    combine = (local_slots[:, :, None] == slot_ids[None, None, :]).astype(bf16)
    moe_sum = jnp.einsum("tec,ehcd->thd", combine, returned, preferred_element_type=f32)
    moe_out = moe_sum.reshape(tok_rows, model_width).astype(bf16)

    counts = jnp.sum(all_routes[:, 2 * TOP, :sequences], axis=0)
    sequence_range = jnp.arange(sequences, dtype=jnp.int32)
    before = sequence_range[None, :] < sequence_range[:, None]
    starts = jnp.sum(jnp.where(before, counts[None, :], 0.0), axis=1)
    token_start = jnp.sum(jnp.where(seq_hits, starts[None, :], 0.0), axis=1)
    global_index = (
        lax.axis_index(DEVICES) * tok_rows + jnp.arange(tok_rows, dtype=jnp.int32)
    ).astype(f32)
    position = global_index - token_start

    next_stream = (stream_f + moe_out.astype(f32)).astype(bf16)
    normed = rms_rows(next_stream.astype(f32), next_gain).astype(bf16)
    compressed = jnp.dot(normed, kv_down, preferred_element_type=f32)
    latent = rms_rows(compressed, kv_gain).astype(bf16)
    rope_in = jnp.dot(normed, rope_down, preferred_element_type=f32)
    rope_key = rotate(rope_in, position).astype(bf16)
    return (moe_out, latent, rope_key)


def solution(mesh):
    chips_mesh = Mesh(
        mesh.devices.reshape(mesh.shape["expert"], mesh.shape["mp"] // 2, 2), DEVICES
    )
    split = P(DEVICES)
    in_specs = (split, P(), split, split, split, split, split, split, P(), P(), P(), P(), P())
    return jax.shard_map(
        local, mesh=chips_mesh, in_specs=in_specs, out_specs=(split,) * 3, check_vma=False
    )
```

time: 918 us -> 479 us (0.52)
  blocking collectives: 341 us -> 44.8 us
  other arithmetic: 306 us -> 10.8 us
  waiting for transfers between devices: 5.32 us -> 174 us
  Pallas kernels: 0 us -> 139 us
  local copies, waits for them, and re-layouts: 142 us -> 4.13 us
  matrix products: 104 us -> 84.4 us
    another operation x38 -> x2, other arithmetic: 259 us -> 2.76 us  [the longest x1 2.6 us: local(): jnp.stack([jnp.where(core == 0, rows_mine, rows_other), jnp.where(core ==...]
    all_to_all x1 -> x0, blocking collectives: 214 us -> none  [local(): lax.all_to_all(outgoing, ('expert', 'mp'), split_axis=0, concat_axis=0, t...]
    pallas_call x0 -> x1, Pallas kernels: none -> 139 us  [damped_solve(): pl.pallas_call(solve_kernel, out_shape=jax.ShapeDtypeStruct((size, width)...]
    psum x1 -> x0, blocking collectives: 127 us -> none  [local(): counts = lax.psum(local_counts, ('expert', 'mp'))]
    all_to_all x1, waiting for transfers between devices: 0.01 us -> 105 us  [local(): lax.all_to_all(outgoing, DEVICES, split_axis=0, concat_axis=0, tiled=True)]
    all_gather x0 -> x1, waiting for transfers between devices: none -> 68.8 us  [local(): lax.all_gather(moe_input, CHIPS, tiled=True)]
    gather x6 -> x0, local copies, waits for them, and re-layouts: 60.8 us -> none  [the longest x1 17.3 us: local(): damping_term = DAMPING * jnp.mean(jnp.diagonal(inner_gram))]
    another operation x44 -> x0, matrix products: 53 us -> none  [the longest x30 29.7 us: local(): jax.scipy.linalg.cho_solve((factor, True), target_cols).astype(jnp.bfloat16)]
  transfers between devices with their start and end apart: 2 -> 5, of which waited for: 1 -> 2; matrix products, arithmetic and copies ran while one was open for 0% -> 8% of each run, Pallas kernels for 0% -> 0%
where the time goes in v1:
time: 479 us; the launch traced here: 476 us
  waiting for transfers between devices  174 us (36%)
  Pallas kernels  139 us (29%)
  matrix products  84.4 us (18%)
  blocking collectives  44.8 us (9%)
  between operations  14.6 us (3%)
  other arithmetic  10.8 us (2%)
    pallas_call x1, Pallas kernels, damped_solve(): pl.pallas_call(solve_kernel, out_shape=jax.ShapeDtypeStruct((size, width)...  139 us
    all_to_all x1, waiting for transfers between devices, local(): lax.all_to_all(outgoing, DEVICES, split_axis=0, concat_axis=0, tiled=True)  105 us
    all_gather x1, waiting for transfers between devices, local(): lax.all_gather(moe_input, CHIPS, tiled=True)  68.8 us
    all_gather x1, blocking collectives, local(): all_routes = lax.all_gather(packed_routes, DEVICES)  44.8 us
    dot_general x1, matrix products, local(): up_proj = jnp.dot(picked, up_full, preferred_element_type=f32)  17.5 us
    dot_general x1, matrix products, local(): gate_proj = jnp.dot(picked, gate_full, preferred_element_type=f32)  14.4 us
    dot_general x2, matrix products, local(): cross_gram = gram(kept_mine, hidden_mine) + gram(kept_other, hidden_other)  10.7 us
  transfers between devices with their start and end apart: 5, of which 2 were waited for; matrix products, arithmetic and copies ran while one was open for 8% of the time, Pallas kernels for 0%

profile of v1, /device:TPU:0, one launch (start us, length us, event | category | flops | bytes accessed | tf_op | source)
XLA Modules:
  0.0 476.0 jit_solution(7443927348771965754)
XLA Ops:
  7.2 0.0 copy-start
  7.2 0.0 all-gather.4.cloned.1.call-start
  7.2 1.4 fusion.31
  8.6 2.0 fusion.33
  10.6 0.0 all-gather.4.cloned.1.call-update
  10.7 0.5 collective-permute-start
  11.2 0.1 collective-permute-start.1
  11.3 0.8 convert_reduce_fusion
  12.0 0.7 convert_bitcast_fusion
  12.7 0.7 maximum_bitcast_fusion
  13.4 44.8 %all-gather.1 = f32[32,13,128]{2,1,0:T(8,128)S(1)} all-gather(f32[1,13,128]{2,1,0:T(8,128)S(1)} %maximum_bitcast_fusion), channel_id=2, replica_groups=mesh['expert'=8,'y'=2,'core'=2] {'expert','y','core'}, dimensions={0}, use_global_device_ids=true | all-gather | bytes 219648 | tf_op jit(solution)/shard_map/all_gather | solution.py:216
  58.2 0.1 fusion.42
  58.3 0.1 reduce_or.19
  58.4 0.1 convolution_select_fusion
  58.5 68.8 %all-gather.4.cloned.1.call-done = bf16[2048,2048]{1,0:T(8,128)(2,1)} async-done(((bf16[128,2048]{1,0:T(8,128)(2,1)}), bf16[2048,2048]{1,0:T(8,128)(2,1)}) %all-gather.4.cloned.1.call-update) | async-done | bytes 8388624 | tf_op jit(solution)/shard_map/all_gather | solution.py:205
  127.3 5.0 %convolution_convert_fusion = bf16[16,72,2048]{2,1,0:T(8,128)(2,1)S(1)} fusion(bf16[16,128,2048]{2,1,0:T(8,128)(2,1)} %bitcast.64, f32[16,128]{1,0:T(8,128)S(1)} %bitcast.71, f32[72]{0:T(128)S(1)} %iota_convert_fusion), kind=kOutput, calls=%fused_computation.25 | convolution fusion | flops 606486528 | bytes 13115680 | tf_op jit(solution)/shard_map/bct,btd->bcd/dot_general | solution.py:231
  132.2 0.0 copy-start.1
  132.3 0.0 collective-permute-done
  132.3 0.0 copy-done.7
  132.3 14.4 %fusion = f32[1152,1408]{1,0:T(8,128)} fusion(bf16[1152,2048]{1,0:T(8,128)(2,1)S(1)} %bitcast.67, bf16[2048,704]{0,1:T(8,128)(2,1)} %collective-permute-done, bf16[2048,704]{0,1:T(8,128)(2,1)S(1)} %bitcast.82, pred[]{:T(512)S(6)} %eq.54), kind=kOutput, calls=%fused_computation.2 | convolution fusion | flops 6669729792 | bytes 16973824 | tf_op jit(solution)/shard_map/dot_general | solution.py:233
  146.6 0.0 copy-done.1
  146.6 0.0 collective-permute-done.1
  146.6 17.5 %multiply_convert_fusion = bf16[1152,1408]{1,0:T(8,128)(2,1)} fusion(f32[1152,1408]{1,0:T(8,128)} %fusion, bf16[1152,2048]{1,0:T(8,128)(2,1)} %bitcast.68, bf16[2048,704]{0,1:T(8,128)(2,1)} %collective-permute-done.1, bf16[2048,704]{0,1:T(8,128)(2,1)} %bitcast.84, pred[]{:T(512)S(6)} %eq.54), kind=kOutput, calls=%fused_computation | convolution fusion | flops 6679461888 | bytes 20217856 | tf_op jit(solution)/shard_map/dot_general | solution.py:234
  164.1 0.0 collective-permute-start.2
  164.2 0.7 fusion.36
  164.8 0.1 mul.142
  164.9 0.1 mul.139
  165.0 0.8 constant_dynamic-slice_fusion.3
  165.8 6.6 %fusion.16 = bf16[1152,1024]{1,0:T(8,128)(2,1)S(1)} fusion(bf16[1152,1408]{1,0:T(8,128)(2,1)} %multiply_convert_fusion, s32[1024]{0:T(1024)S(1)} %bitcast.78), kind=kOutput, calls=%fused_computation.26 | convolution fusion | flops 3324510208 | bytes 5607424 | tf_op jit(solution)/shard_map/dot_general | solution.py:241
  172.4 0.0 copy-start.6
  172.4 3.0 fusion.59
  175.4 0.0 copy-done.6
  175.4 4.4 fusion.60
  179.8 0.0 collective-permute-done.2
  179.8 6.2 %fusion.17 = bf16[1152,1024]{1,0:T(8,128)(2,1)S(1)} fusion(bf16[1152,1408]{1,0:T(8,128)(2,1)} %collective-permute-done.2, s32[1024]{0:T(1024)S(1)} %bitcast.79), kind=kOutput, calls=%fused_computation.27 | convolution fusion | flops 3324510208 | bytes 5607424 | tf_op jit(solution)/shard_map/dot_general | solution.py:242
  186.0 6.3 %fusion.58 = (bf16[1024,1408]{1,0:T(8,128)(2,1)S(1)}, f32[1024,1408]{1,0:T(8,128)S(1)}) fusion(f32[1024,1408]{1,0:T(8,128)S(1)} %fusion.60, bf16[1152,1024]{1,0:T(8,128)(2,1)S(1)} %fusion.17, bf16[1152,1408]{1,0:T(8,128)(2,1)} %collective-permute-done.2), kind=kOutput, calls=%fused_computation.108 | convolution fusion | flops 3324772352 | bytes 20021248 | tf_op jit(solution)/shard_map/dot_general | solution.py:247
  192.3 0.0 copy-done
  192.3 3.5 fusion.18
  195.8 5.0 %fusion.25.target_ref = f32[1024,1024]{1,0:T(8,128)} fusion(f32[1024,1024]{1,0:T(8,128)S(1)} %fusion.18, bf16[1024,1408]{1,0:T(8,128)(2,1)S(1)} %get-tuple-element.15, bf16[1,1408,1024]{2,1,0:T(8,128)(2,1)S(1)} %copy-done), kind=kOutput, calls=%fused_computation.40 | convolution fusion | flops 2953838592 | bytes 14155776 | tf_op jit(solution)/shard_map/dot_general | solution.py:163
  200.9 4.5 convolution_add_fusion.1.inner_ref
  205.3 138.6 %shard_map.148 = bf16[1024,1024]{1,0:T(8,128)(2,1)S(1)} custom-call(f32[1024,1024]{1,0:T(8,128)} %convolution_add_fusion.1.inner_ref, f32[1024,1024]{1,0:T(8,128)} %fusion.25.target_ref), custom_call_target="tpu_custom_call" | custom-call | flops 6442450944 | bytes 10485760 | tf_op jit(solution)/shard_map/pallas_call | solution.py:144
  344.0 2.8 multiply_convert_fusion.1
  346.8 3.0 broadcast_select_fusion.1
  349.8 2.6 pad_maximum_fusion
  352.4 3.7 all-to-all-start
  356.2 0.1 slice_reduce_fusion
  356.2 0.1 select_reduce_fusion.2
  356.4 0.1 select_reduce_fusion.1
  356.5 0.1 convolution_select_fusion.1
  356.6 105.5 %all-to-all-done = bf16[32,72,1024]{2,1,0:T(8,128)(2,1)} async-done(((bf16[32,72,1024]{2,1,0:T(8,128)(2,1)}), bf16[32,72,1024]{2,1,0:T(8,128)(2,1)}, u32[]{:S(2)}, u32[]{:S(2)}) %all-to-all-start) | async-done | bytes 4718624 | tf_op jit(solution)/shard_map/all_to_all | solution.py:267
  462.1 2.9 copy.28
  465.0 0.0 copy-start.9
  465.1 0.0 copy-start.10
  465.1 0.0 copy-start.8
  465.1 1.1 fusion.28
  466.2 0.0 copy-start.3
  466.2 0.0 copy-start.5
  466.2 0.4 fusion.54
  466.6 0.1 copy-done.8
  466.8 0.6 multiply_reduce_fusion
  467.3 0.2 fusion.49
  467.5 0.6 pad_maximum_fusion.1
  468.1 0.7 multiply_convert_fusion.3
  468.9 0.0 copy-done.3
  (20 shorter events, 0.1 us)
Async XLA Ops:
  7.2 185.2 %copy-start = (bf16[1,1408,1024]{2,1,0:T(8,128)(2,1)S(1)}, bf16[1,1408,1024]{2,1,0:T(8,128)(2,1)}, u32[]{:S(2)}) copy-start(bf16[1,1408,1024]{2,1,0:T(8,128)(2,1)} %param.20) | copy-start | bytes 8650756
  7.2 120.1 %all-gather.4.cloned.1.call-start = ((), (), s32[]{:S(2)}) async-start(), calls=%async_computation.1 | async-start | bytes 8912896 | tf_op jit(solution)/shard_map/all_gather | solution.py:205
  10.7 121.6 %collective-permute-start = (bf16[2048,704]{0,1:T(8,128)(2,1)}, bf16[2048,704]{0,1:T(8,128)(2,1)}, u32[]{:S(2)}, u32[]{:S(2)}) collective-permute-start(bf16[2048,704]{0,1:T(8,128)(2,1)} %bitcast.81), channel_id=1, source_target_pairs={{0,1},{1,0},{2,3},{3,2},{4,5},{5,4},{6,7},{7,6},{8,9},{9,8},{10,11... | collective-permute-start | bytes 8650760 | tf_op jit(solution)/shard_map/ppermute | solution.py:169
  11.2 135.5 %collective-permute-start.1 = (bf16[2048,704]{0,1:T(8,128)(2,1)}, bf16[2048,704]{0,1:T(8,128)(2,1)}, u32[]{:S(2)}, u32[]{:S(2)}) collective-permute-start(bf16[2048,704]{0,1:T(8,128)(2,1)} %bitcast.83), channel_id=1, source_target_pairs={{0,1},{1,0},{2,3},{3,2},{4,5},{5,4},{6,7},{7,6},{8,9},{9,8},{10,11... | collective-permute-start | bytes 8650760 | tf_op jit(solution)/shard_map/ppermute | solution.py:169
  127.3 5.0 %copy-start.7 = (bf16[1,2048,704]{1,2,0:T(8,128)(2,1)S(1)}, bf16[1,2048,704]{1,2,0:T(8,128)(2,1)}, u32[]{:S(2)}) copy-start(bf16[1,2048,704]{1,2,0:T(8,128)(2,1)} %param.18) | copy-start | bytes 8650756
  132.2 14.4 %copy-start.1 = (bf16[16,72,2048]{2,1,0:T(8,128)(2,1)}, bf16[16,72,2048]{2,1,0:T(8,128)(2,1)S(1)}, u32[]{:S(2)}) copy-start(bf16[16,72,2048]{2,1,0:T(8,128)(2,1)S(1)} %convolution_convert_fusion) | copy-start | bytes 14155780
  164.1 15.6 %collective-permute-start.2 = (bf16[1152,1408]{1,0:T(8,128)(2,1)}, bf16[1152,1408]{1,0:T(8,128)(2,1)}, u32[]{:S(2)}, u32[]{:S(2)}) collective-permute-start(bf16[1152,1408]{1,0:T(8,128)(2,1)} %multiply_convert_fusion), channel_id=1, source_target_pairs={{0,1},{1,0},{2,3},{3,2},{4,5},{5,4},{6,7},{7,6},{8,9},{9,8},{10,11... | collective-permute-start | bytes 9732104 | tf_op jit(solution)/shard_map/ppermute | solution.py:236
  172.4 3.0 copy-start.6
  352.4 3.9 copy-start.4
  352.4 3.9 copy-start.11
  352.4 109.6 %all-to-all-start = ((bf16[32,72,1024]{2,1,0:T(8,128)(2,1)}), bf16[32,72,1024]{2,1,0:T(8,128)(2,1)}, u32[]{:S(2)}, u32[]{:S(2)}) async-start(bf16[32,72,1024]{2,1,0:T(8,128)(2,1)} %bitcast.65), calls=%async_computation | async-start | bytes 9437184 | tf_op jit(solution)/shard_map/all_to_all | solution.py:267
  462.1 3.0 copy-start.2
  465.0 1.1 copy-start.9
  465.1 1.1 copy-start.10
  465.1 1.7 copy-start.8
  466.2 2.7 copy-start.3
  466.2 1.9 copy-start.5
Sparse Core Ops, SparseCore 0:
  11.3 115.9 all-gather.3

commit v2 on v1

--- a/solution.py
+++ b/solution.py
@@ -80,7 +80,14 @@
     return tuple(pltpu.roll(row, BLOCK - SUB, 1) for row in out)
 
 
-def solve_kernel(inner_ref, target_ref, out_ref, work, gain):
+def in_three(value):
+    high = value.astype(jnp.bfloat16)
+    rest = value - high.astype(jnp.float32)
+    middle = rest.astype(jnp.bfloat16)
+    return high, middle, (rest - middle.astype(jnp.float32)).astype(jnp.bfloat16)
+
+
+def solve_kernel(inner_ref, target_ref, out_ref, work, near, far):
     size = inner_ref.shape[0]
     width = target_ref.shape[1]
     blocks = size // BLOCK
@@ -100,43 +107,71 @@
         work[at, :size] = inner_ref[at, :] * scale
         work[at, size:] = target_ref[at, :] * scale
 
+    def diagonal_rows(k):
+        at = pl.ds(k * BLOCK, BLOCK)
+        square = work[at, at] + jnp.where(eye, DAMPING, 0.0)
+        return tuple(square[SUB * i : SUB * (i + 1), :] for i in range(BLOCK // SUB))
+
+    def two_steps(rows):
+        return sweep_step(sweep_step(rows))
+
+    pairs = BLOCK // SUB // 2
+    rows = lax.fori_loop(0, pairs, lambda _, rows: two_steps(rows), diagonal_rows(0))
     for k in range(blocks):
         at = pl.ds(k * BLOCK, BLOCK)
         low = (k + 1) * BLOCK
-        square = work[at, at] + jnp.where(eye, DAMPING, 0.0)
-        rows = tuple(square[SUB * i : SUB * (i + 1), :] for i in range(BLOCK // SUB))
-        rows = lax.fori_loop(0, BLOCK // SUB, lambda _, rows: sweep_step(rows), rows)
         inverse = jnp.concatenate(rows, axis=0)
-        tile = 512 if low % 512 == 0 else (256 if low % 256 == 0 else BLOCK)
-
-        def column(start, tile, low=low, at=at, inverse=inverse):
+        high, middle, small = in_three(work[:, at])
+        near[:, :BLOCK] = high
+        near[:, BLOCK:] = middle
+        far[:, :BLOCK] = high
+        far[:, BLOCK:] = small
+        ranges = [r for r in ((0, k * BLOCK), (low, size)) if r[0] < r[1]]
+
+        def column(start, tile, at=at, inverse=inverse, ranges=ranges):
             cols = pl.ds(start, tile)
             solved = precise_dot(inverse, work[at, cols])
-            gain[at, cols] = solved
-            if low < size:
-                work[low:, cols] -= precise_dot(work[low:, at], solved)
-
-        start = low
-        while start % 512:
+            b0, b1, b2 = in_three(solved)
+            b00 = jnp.concatenate([b0, b0], axis=0)
+            b11 = jnp.concatenate([b1, b1], axis=0)
+            b20 = jnp.concatenate([b2, b0], axis=0)
+            for first, last in ranges:
+                change = jnp.dot(near[first:last], b00, preferred_element_type=jnp.float32)
+                change += jnp.dot(near[first:last], b11, preferred_element_type=jnp.float32)
+                change += jnp.dot(far[first:last], b20, preferred_element_type=jnp.float32)
+                work[first:last, cols] -= change
+            work[at, cols] = solved
+
+        start, tiles = low, 0
+        if k + 1 < blocks:
             column(start, BLOCK)
             start += BLOCK
-
-        @pl.loop(0, (size + width - start) // 512)
+            rows = diagonal_rows(k + 1)
+        if start % 256:
+            column(start, BLOCK)
+            start += BLOCK
+        tiles = (size + width - start) // 256
+
+        if k + 1 < blocks:
+            beside = min(tiles, pairs)
+
+            def body(i, rows, start=start, column=column):
+                column(pl.multiple_of(start + i * 256, 256), 256)
+                return two_steps(rows)
+
+            rows = lax.fori_loop(0, beside, body, rows)
+            rows = lax.fori_loop(beside, pairs, lambda _, rows: two_steps(rows), rows)
+        else:
+            beside = 0
+
+        @pl.loop(beside, tiles)
         def _(i, start=start, column=column):
-            column(pl.multiple_of(start + i * 512, 512), 512)
-
-    @pl.loop(0, width // 256)
+            column(pl.multiple_of(start + i * 256, 256), 256)
+
+    @pl.loop(0, size // 32)
     def _(i):
-        start = pl.multiple_of(i * 256, 256)
-        cols = pl.ds(pl.multiple_of(size + start, 256), 256)
-        for k in reversed(range(blocks)):
-            at = pl.ds(k * BLOCK, BLOCK)
-            low = (k + 1) * BLOCK
-            value = gain[at, cols]
-            if low < size:
-                value = value - precise_dot(gain[at, low:size], work[low:, cols])
-            work[at, cols] = value
-        out_ref[:, pl.ds(start, 256)] = work[:, cols].astype(out_ref.dtype)
+        at = pl.ds(pl.multiple_of(i * 32, 32), 32)
+        out_ref[at, :] = work[at, size:].astype(out_ref.dtype)
 
 
 def damped_solve(inner, target):
@@ -148,7 +183,8 @@
         out_specs=pl.BlockSpec(memory_space=pltpu.VMEM),
         scratch_shapes=[
             pltpu.VMEM((size, size + width), jnp.float32),
-            pltpu.VMEM((size, size + width), jnp.float32),
+            pltpu.VMEM((size, 2 * BLOCK), jnp.bfloat16),
+            pltpu.VMEM((size, 2 * BLOCK), jnp.bfloat16),
         ],
         compiler_params=pltpu.CompilerParams(vmem_limit_bytes=48 * 2**20),
         cost_estimate=pl.CostEstimate(

time: 479 us -> 437 us (0.912)
  Pallas kernels: 139 us -> 96.9 us
    pallas_call x1, Pallas kernels: 139 us -> 96.9 us  [damped_solve(): pl.pallas_call(solve_kernel, out_shape=jax.ShapeDtypeStruct((size, width)...]
  transfers between devices with their start and end apart: 5 -> 5, of which waited for: 2 -> 2; matrix products, arithmetic and copies ran while one was open for 8% -> 9% of each run, Pallas kernels for 0% -> 0%
where the time goes in v2:
time: 437 us; the launch traced here: 434 us
  waiting for transfers between devices  174 us (40%)
  Pallas kernels  96.9 us (22%)
  matrix products  84.4 us (19%)
  blocking collectives  44.8 us (10%)
  between operations  14.6 us (3%)
  other arithmetic  10.8 us (2%)
    all_to_all x1, waiting for transfers between devices, local(): lax.all_to_all(outgoing, DEVICES, split_axis=0, concat_axis=0, tiled=True)  105 us
    pallas_call x1, Pallas kernels, damped_solve(): pl.pallas_call(solve_kernel, out_shape=jax.ShapeDtypeStruct((size, width)...  96.9 us
    all_gather x1, waiting for transfers between devices, local(): lax.all_gather(moe_input, CHIPS, tiled=True)  68.8 us
    all_gather x1, blocking collectives, local(): all_routes = lax.all_gather(packed_routes, DEVICES)  44.8 us
    dot_general x1, matrix products, local(): up_proj = jnp.dot(picked, up_full, preferred_element_type=f32)  17.5 us
    dot_general x1, matrix products, local(): gate_proj = jnp.dot(picked, gate_full, preferred_element_type=f32)  14.4 us
    dot_general x2, matrix products, local(): cross_gram = gram(kept_mine, hidden_mine) + gram(kept_other, hidden_other)  10.7 us
  transfers between devices with their start and end apart: 5, of which 2 were waited for; matrix products, arithmetic and copies ran while one was open for 9% of the time, Pallas kernels for 0%

profile of v2, /device:TPU:0, one launch (start us, length us, event | category | flops | bytes accessed | tf_op | source)
XLA Modules:
  0.0 434.2 jit_solution(766496115335119285)
XLA Ops:
  7.2 0.0 copy-start
  7.2 0.0 all-gather.4.cloned.1.call-start
  7.2 1.4 fusion.31
  8.6 2.0 fusion.33
  10.6 0.0 all-gather.4.cloned.1.call-update
  10.7 0.5 collective-permute-start
  11.2 0.1 collective-permute-start.1
  11.3 0.8 convert_reduce_fusion
  12.0 0.7 convert_bitcast_fusion
  12.7 0.7 maximum_bitcast_fusion
  13.4 44.8 %all-gather.1 = f32[32,13,128]{2,1,0:T(8,128)S(1)} all-gather(f32[1,13,128]{2,1,0:T(8,128)S(1)} %maximum_bitcast_fusion), channel_id=2, replica_groups=mesh['expert'=8,'y'=2,'core'=2] {'expert','y','core'}, dimensions={0}, use_global_device_ids=true | all-gather | bytes 219648 | tf_op jit(solution)/shard_map/all_gather | solution.py:252
  58.2 0.1 fusion.42
  58.3 0.1 reduce_or.19
  58.4 0.1 convolution_select_fusion
  58.5 68.8 %all-gather.4.cloned.1.call-done = bf16[2048,2048]{1,0:T(8,128)(2,1)} async-done(((bf16[128,2048]{1,0:T(8,128)(2,1)}), bf16[2048,2048]{1,0:T(8,128)(2,1)}) %all-gather.4.cloned.1.call-update) | async-done | bytes 8388624 | tf_op jit(solution)/shard_map/all_gather | solution.py:241
  127.3 5.0 %convolution_convert_fusion = bf16[16,72,2048]{2,1,0:T(8,128)(2,1)S(1)} fusion(bf16[16,128,2048]{2,1,0:T(8,128)(2,1)} %bitcast.64, f32[16,128]{1,0:T(8,128)S(1)} %bitcast.71, f32[72]{0:T(128)S(1)} %iota_convert_fusion), kind=kOutput, calls=%fused_computation.25 | convolution fusion | flops 606486528 | bytes 13115680 | tf_op jit(solution)/shard_map/bct,btd->bcd/dot_general | solution.py:267
  132.2 0.0 copy-start.1
  132.3 0.0 collective-permute-done
  132.3 0.0 copy-done.7
  132.3 14.4 %fusion = f32[1152,1408]{1,0:T(8,128)} fusion(bf16[1152,2048]{1,0:T(8,128)(2,1)S(1)} %bitcast.67, bf16[2048,704]{0,1:T(8,128)(2,1)} %collective-permute-done, bf16[2048,704]{0,1:T(8,128)(2,1)S(1)} %bitcast.82, pred[]{:T(512)S(6)} %eq.54), kind=kOutput, calls=%fused_computation.2 | convolution fusion | flops 6669729792 | bytes 16973824 | tf_op jit(solution)/shard_map/dot_general | solution.py:269
  146.6 0.0 copy-done.1
  146.6 0.0 collective-permute-done.1
  146.6 17.5 %multiply_convert_fusion = bf16[1152,1408]{1,0:T(8,128)(2,1)} fusion(f32[1152,1408]{1,0:T(8,128)} %fusion, bf16[1152,2048]{1,0:T(8,128)(2,1)} %bitcast.68, bf16[2048,704]{0,1:T(8,128)(2,1)} %collective-permute-done.1, bf16[2048,704]{0,1:T(8,128)(2,1)} %bitcast.84, pred[]{:T(512)S(6)} %eq.54), kind=kOutput, calls=%fused_computation | convolution fusion | flops 6679461888 | bytes 20217856 | tf_op jit(solution)/shard_map/dot_general | solution.py:270
  164.1 0.0 collective-permute-start.2
  164.2 0.7 fusion.36
  164.8 0.1 mul.142
  164.9 0.1 mul.139
  165.0 0.8 constant_dynamic-slice_fusion.3
  165.8 6.6 %fusion.16 = bf16[1152,1024]{1,0:T(8,128)(2,1)S(1)} fusion(bf16[1152,1408]{1,0:T(8,128)(2,1)} %multiply_convert_fusion, s32[1024]{0:T(1024)S(1)} %bitcast.78), kind=kOutput, calls=%fused_computation.26 | convolution fusion | flops 3324510208 | bytes 5607424 | tf_op jit(solution)/shard_map/dot_general | solution.py:277
  172.4 0.0 copy-start.6
  172.4 3.0 fusion.59
  175.4 0.0 copy-done.6
  175.4 4.4 %fusion.60 = f32[1024,1408]{1,0:T(8,128)S(1)} fusion(bf16[1152,1024]{1,0:T(8,128)(2,1)S(1)} %fusion.16, bf16[1152,1408]{1,0:T(8,128)(2,1)S(1)} %copy-done.6), kind=kOutput, calls=%fused_computation.110 | convolution fusion | flops 3321888768 | bytes 11370496 | tf_op jit(solution)/shard_map/dot_general | solution.py:283
  179.8 0.0 collective-permute-done.2
  179.8 6.2 %fusion.17 = bf16[1152,1024]{1,0:T(8,128)(2,1)S(1)} fusion(bf16[1152,1408]{1,0:T(8,128)(2,1)} %collective-permute-done.2, s32[1024]{0:T(1024)S(1)} %bitcast.79), kind=kOutput, calls=%fused_computation.27 | convolution fusion | flops 3324510208 | bytes 5607424 | tf_op jit(solution)/shard_map/dot_general | solution.py:278
  186.0 6.3 %fusion.58 = (bf16[1024,1408]{1,0:T(8,128)(2,1)S(1)}, f32[1024,1408]{1,0:T(8,128)S(1)}) fusion(f32[1024,1408]{1,0:T(8,128)S(1)} %fusion.60, bf16[1152,1024]{1,0:T(8,128)(2,1)S(1)} %fusion.17, bf16[1152,1408]{1,0:T(8,128)(2,1)} %collective-permute-done.2), kind=kOutput, calls=%fused_computation.108 | convolution fusion | flops 3324772352 | bytes 20021248 | tf_op jit(solution)/shard_map/dot_general | solution.py:283
  192.3 3.5 fusion.18
  195.8 5.0 %fusion.25.target_ref = f32[1024,1024]{1,0:T(8,128)} fusion(f32[1024,1024]{1,0:T(8,128)S(1)} %fusion.18, bf16[1024,1408]{1,0:T(8,128)(2,1)S(1)} %get-tuple-element.15, bf16[1,1408,1024]{2,1,0:T(8,128)(2,1)S(1)} %copy-done), kind=kOutput, calls=%fused_computation.40 | convolution fusion | flops 2953838592 | bytes 14155776 | tf_op jit(solution)/shard_map/dot_general | solution.py:199
  200.9 4.5 %convolution_add_fusion.1.inner_ref = f32[1024,1024]{1,0:T(8,128)} fusion(f32[1024,1024]{1,0:T(8,128)S(1)} %fusion.59, bf16[1152,1024]{1,0:T(8,128)(2,1)S(1)} %fusion.17), kind=kOutput, calls=%fused_computation.41 | convolution fusion | flops 2416967680 | bytes 10747904 | tf_op jit(solution)/shard_map/dot_general | solution.py:284
  205.3 96.9 %shard_map.148 = bf16[1024,1024]{1,0:T(8,128)(2,1)S(1)} custom-call(f32[1024,1024]{1,0:T(8,128)} %convolution_add_fusion.1.inner_ref, f32[1024,1024]{1,0:T(8,128)} %fusion.25.target_ref), custom_call_target="tpu_custom_call" | custom-call | flops 6442450944 | bytes 10485760 | tf_op jit(solution)/shard_map/pallas_call | solution.py:179
  302.2 2.8 multiply_convert_fusion.1
  305.0 3.0 broadcast_select_fusion.1
  308.1 2.6 pad_maximum_fusion
  310.7 3.7 all-to-all-start
  314.4 0.1 slice_reduce_fusion
  314.5 0.1 select_reduce_fusion.2
  314.6 0.1 select_reduce_fusion.1
  314.7 0.1 convolution_select_fusion.1
  314.9 105.5 %all-to-all-done = bf16[32,72,1024]{2,1,0:T(8,128)(2,1)} async-done(((bf16[32,72,1024]{2,1,0:T(8,128)(2,1)}), bf16[32,72,1024]{2,1,0:T(8,128)(2,1)}, u32[]{:S(2)}, u32[]{:S(2)}) %all-to-all-start) | async-done | bytes 4718624 | tf_op jit(solution)/shard_map/all_to_all | solution.py:303
  420.4 2.9 copy.28
  423.3 0.0 copy-start.9
  423.3 0.0 copy-start.10
  423.3 0.0 copy-start.8
  423.4 1.1 fusion.28
  424.4 0.0 copy-start.3
  424.4 0.0 copy-start.5
  424.5 0.0 copy-done.9
  424.5 0.0 copy-done.10
  424.5 0.4 fusion.54
  424.9 0.1 copy-done.8
  425.0 0.6 multiply_reduce_fusion
  425.6 0.2 fusion.49
  425.8 0.6 pad_maximum_fusion.1
  426.4 0.7 multiply_convert_fusion.3
  (20 shorter events, 0.1 us)
Async XLA Ops:
  7.2 185.2 %copy-start = (bf16[1,1408,1024]{2,1,0:T(8,128)(2,1)S(1)}, bf16[1,1408,1024]{2,1,0:T(8,128)(2,1)}, u32[]{:S(2)}) copy-start(bf16[1,1408,1024]{2,1,0:T(8,128)(2,1)} %param.20) | copy-start | bytes 8650756
  7.2 120.1 %all-gather.4.cloned.1.call-start = ((), (), s32[]{:S(2)}) async-start(), calls=%async_computation.1 | async-start | bytes 8912896 | tf_op jit(solution)/shard_map/all_gather | solution.py:241
  10.7 121.6 %collective-permute-start = (bf16[2048,704]{0,1:T(8,128)(2,1)}, bf16[2048,704]{0,1:T(8,128)(2,1)}, u32[]{:S(2)}, u32[]{:S(2)}) collective-permute-start(bf16[2048,704]{0,1:T(8,128)(2,1)} %bitcast.81), channel_id=1, source_target_pairs={{0,1},{1,0},{2,3},{3,2},{4,5},{5,4},{6,7},{7,6},{8,9},{9,8},{10,11... | collective-permute-start | bytes 8650760 | tf_op jit(solution)/shard_map/ppermute | solution.py:205
  11.2 135.5 %collective-permute-start.1 = (bf16[2048,704]{0,1:T(8,128)(2,1)}, bf16[2048,704]{0,1:T(8,128)(2,1)}, u32[]{:S(2)}, u32[]{:S(2)}) collective-permute-start(bf16[2048,704]{0,1:T(8,128)(2,1)} %bitcast.83), channel_id=1, source_target_pairs={{0,1},{1,0},{2,3},{3,2},{4,5},{5,4},{6,7},{7,6},{8,9},{9,8},{10,11... | collective-permute-start | bytes 8650760 | tf_op jit(solution)/shard_map/ppermute | solution.py:205
  127.3 5.0 %copy-start.7 = (bf16[1,2048,704]{1,2,0:T(8,128)(2,1)S(1)}, bf16[1,2048,704]{1,2,0:T(8,128)(2,1)}, u32[]{:S(2)}) copy-start(bf16[1,2048,704]{1,2,0:T(8,128)(2,1)} %param.18) | copy-start | bytes 8650756
  132.2 14.4 %copy-start.1 = (bf16[16,72,2048]{2,1,0:T(8,128)(2,1)}, bf16[16,72,2048]{2,1,0:T(8,128)(2,1)S(1)}, u32[]{:S(2)}) copy-start(bf16[16,72,2048]{2,1,0:T(8,128)(2,1)S(1)} %convolution_convert_fusion) | copy-start | bytes 14155780
  164.1 15.6 %collective-permute-start.2 = (bf16[1152,1408]{1,0:T(8,128)(2,1)}, bf16[1152,1408]{1,0:T(8,128)(2,1)}, u32[]{:S(2)}, u32[]{:S(2)}) collective-permute-start(bf16[1152,1408]{1,0:T(8,128)(2,1)} %multiply_convert_fusion), channel_id=1, source_target_pairs={{0,1},{1,0},{2,3},{3,2},{4,5},{5,4},{6,7},{7,6},{8,9},{9,8},{10,11... | collective-permute-start | bytes 9732104 | tf_op jit(solution)/shard_map/ppermute | solution.py:272
  172.4 3.0 copy-start.6
  310.7 3.9 copy-start.4
  310.7 3.9 copy-start.11
  310.7 109.6 %all-to-all-start = ((bf16[32,72,1024]{2,1,0:T(8,128)(2,1)}), bf16[32,72,1024]{2,1,0:T(8,128)(2,1)}, u32[]{:S(2)}, u32[]{:S(2)}) async-start(bf16[32,72,1024]{2,1,0:T(8,128)(2,1)} %bitcast.65), calls=%async_computation | async-start | bytes 9437184 | tf_op jit(solution)/shard_map/all_to_all | solution.py:303
  420.4 3.0 copy-start.2
  423.3 1.1 copy-start.9
  423.3 1.1 copy-start.10
  423.3 1.7 copy-start.8
  424.4 2.7 copy-start.3
  424.4 1.9 copy-start.5
Sparse Core Ops, SparseCore 0:
  11.3 115.9 all-gather.3
